TPU v7x, 128 devices: a whole 4x4x4 slice. The times are simulated.
128 devices in a mesh: tp: 2 (over core), grp: 32 (over z, y, x_lo), rep: 2 (over x_hi).
Axes of the slice: x: 4 (x_hi: 2, x_lo: 2; x = x_hi * 2 + x_lo), y: 4, z: 4, core: 2. Of those that a mesh axis runs over, the one named last changes fastest.
Arguments:
- tokens: bfloat16 [8192, 4096], P(('rep', 'tp', 'grp')), parts along dimension 0, may hold values from -6 to 6
- qkv_weight: bfloat16 [4096, 5120], P(None, ('tp', 'grp')), may hold values from -0.09375 to 0.09375
- qkv_bias: bfloat16 [5120], replicated, may hold values from -3 to 3
- cache: bfloat16 [512, 1024, 1024], P(('rep', 'tp', 'grp')), parts along dimension 0, may hold values from -80 to 80
- lengths: int32 [512], P('rep'), parts along dimension 0, may hold values from 128 to 1024, as said below
- slot_stream: int32 [512], P('rep'), parts along dimension 0, may hold values from 0 to 255, each once
Outputs:
- attended: bfloat16 [8192, 4096], P(('rep', 'tp', 'grp')), parts along dimension 0
There are 2 independent parts, one for each index of `rep`. A program takes and returns all parts, laid end to end along the dimension named above; an argument that names none is the same for every part. Nothing has to cross between parts.
Inputs may be any that keep to these rules, and one draw needn't show every extreme that they name: `lengths`: cache length of each stream; some stream has exactly 1024 and some exactly 128. `slot_stream`: each stream appears in exactly one slot.
All inputs are finite; a program needn't handle non-finite values.
Results may differ from a plain program's by a relative error of at most 0.004.
The roundings to bfloat16 on the way count: a program that leaves them out, or rounds other values in their place, can miss the bound.
Values may be sent and summed in bfloat16 or wider, within the bound.
No kernel may reach another device: no remote copies, remote signals or barrier semaphores. Data moves between devices by JAX's collectives and lax.ppermute only.
A program may use at most 128 MiB of HBM per device.

v0:
```python
import jax
import jax.numpy as jnp
from jax import lax
from jax.sharding import PartitionSpec as P

HD = 128
HQ = 32
KVH = 4
STRETCH = 16
CAP = 1024
GROUP = 8
ROPE_THETA = 1000000.0


def rotate(vectors, positions):
    half_width = vectors.shape[-1] // 2
    frequency = ROPE_THETA ** (
        -(jnp.arange(half_width, dtype=jnp.float32) * 2.0) / vectors.shape[-1]
    )
    angles = positions.astype(jnp.float32)[:, None] * frequency[None, :]
    cosine = jnp.cos(angles)[:, None, :]
    sine_part = jnp.sin(angles)[:, None, :]
    front_half = vectors[..., :half_width]
    back_half = vectors[..., half_width:]
    return jnp.concatenate(
        [front_half * cosine - back_half * sine_part, back_half * cosine + front_half * sine_part],
        axis=-1,
    )


def attend(token_block, slot_cache, length):
    query_width = HQ * HD
    kv_width = KVH * HD
    positions = length + jnp.arange(STRETCH, dtype=jnp.int32)
    queries = rotate(
        token_block[:, :query_width].astype(jnp.float32).reshape(STRETCH, HQ, HD), positions
    ).astype(jnp.bfloat16)
    new_keys = rotate(
        token_block[:, query_width : query_width + kv_width]
        .astype(jnp.float32)
        .reshape(STRETCH, KVH, HD),
        positions,
    ).astype(jnp.bfloat16)
    new_values = token_block[:, query_width + kv_width :].reshape(STRETCH, KVH, HD)
    grouped = (
        queries.reshape(STRETCH, KVH, GROUP, HD)
        .transpose(1, 0, 2, 3)
        .reshape(KVH, STRETCH * GROUP, HD)
    )
    score_scale = HD ** (-0.5)
    query_token = jnp.arange(STRETCH * GROUP, dtype=jnp.int32) // GROUP
    scores = (
        jnp.einsum("krd,jkd->krj", grouped, new_keys, preferred_element_type=jnp.float32)
        * score_scale
    )
    causal = jnp.arange(STRETCH, dtype=jnp.int32)[None, :] <= query_token[:, None]
    scores = jnp.where(causal[None], scores, -jnp.inf)
    row_max = jnp.max(scores, axis=-1)
    exponent = jnp.exp(scores - row_max[..., None])
    row_total = jnp.sum(exponent, axis=-1)
    running = jnp.einsum(
        "krj,jkd->krd",
        exponent.astype(jnp.bfloat16),
        new_values,
        preferred_element_type=jnp.float32,
    )
    key_span = min(CAP, 256)
    key_part = slot_cache[:, :kv_width]
    value_part = slot_cache[:, kv_width:]

    def visit(block_index, running_state):
        old_max, old_total, old_sum = running_state
        offset = block_index * key_span
        key_block = lax.dynamic_slice_in_dim(key_part, offset, key_span, 0).reshape(
            key_span, KVH, HD
        )
        value_block = lax.dynamic_slice_in_dim(value_part, offset, key_span, 0).reshape(
            key_span, KVH, HD
        )
        block_scores = (
            jnp.einsum("krd,jkd->krj", grouped, key_block, preferred_element_type=jnp.float32)
            * score_scale
        )
        in_cache = offset + jnp.arange(key_span, dtype=jnp.int32) < length
        block_scores = jnp.where(in_cache[None, None, :], block_scores, -jnp.inf)
        new_max = jnp.maximum(old_max, jnp.max(block_scores, axis=-1))
        rescale = jnp.exp(old_max - new_max)
        block_exp = jnp.exp(block_scores - new_max[..., None])
        new_total = old_total * rescale + jnp.sum(block_exp, axis=-1)
        new_sum = old_sum * rescale[..., None] + jnp.einsum(
            "krj,jkd->krd",
            block_exp.astype(jnp.bfloat16),
            value_block,
            preferred_element_type=jnp.float32,
        )
        return (new_max, new_total, new_sum)

    block_count = CAP // key_span
    row_max, row_total, running = lax.fori_loop(
        0, block_count, visit, (row_max, row_total, running)
    )
    result = running / row_total[..., None]
    return (
        result.reshape(KVH, STRETCH, GROUP, HD)
        .transpose(1, 0, 2, 3)
        .reshape(STRETCH, HQ * HD)
        .astype(jnp.bfloat16)
    )


def on_device(tokens, qkv_weight, qkv_bias, cache, lengths, slot_stream):
    my_index = lax.axis_index(("tp", "grp"))
    grp_index = lax.axis_index("grp")
    tp_count = lax.axis_size("tp")
    grp_count = lax.axis_size("grp")
    per_device = cache.shape[0]
    local_rows = per_device * STRETCH
    shard_cols = qkv_weight.shape[1]
    weight_cols = lax.all_gather(qkv_weight, "tp", axis=1, tiled=True)
    bias_table = qkv_bias.reshape(tp_count, grp_count, shard_cols)
    bias_cols = (
        lax.dynamic_index_in_dim(bias_table, grp_index, 1, keepdims=False)
        .reshape(-1)
        .astype(jnp.float32)
    )
    partial_cols = jnp.dot(
        lax.all_gather(tokens, "grp", axis=0, tiled=True),
        weight_cols,
        preferred_element_type=jnp.float32,
    )
    rounded_cols = (partial_cols + bias_cols[None, :]).astype(jnp.bfloat16)
    received = lax.all_to_all(rounded_cols, "grp", split_axis=0, concat_axis=1, tiled=True)
    projected_qkv = (
        received.reshape(local_rows, grp_count, tp_count, shard_cols)
        .transpose(0, 2, 1, 3)
        .reshape(local_rows, -1)
    )
    my_slots = my_index * per_device + jnp.arange(per_device, dtype=jnp.int32)
    my_lengths = jnp.take(lengths, jnp.take(slot_stream, my_slots))
    attended = jnp.concatenate(
        [
            attend(
                projected_qkv[slot_index * STRETCH : (slot_index + 1) * STRETCH],
                cache[slot_index],
                my_lengths[slot_index],
            )
            for slot_index in range(per_device)
        ],
        axis=0,
    )
    return attended


def solution(mesh):
    in_specs = (
        P(("rep", "tp", "grp"), None),
        P(None, ("tp", "grp")),
        P(),
        P(("rep", "tp", "grp"), None, None),
        P("rep"),
        P("rep"),
    )
    out_specs = P(("rep", "tp", "grp"), None)
    return jax.shard_map(
        on_device, mesh=mesh, in_specs=in_specs, out_specs=out_specs, check_vma=False
    )
```

profile of v0, /device:TPU:0, one launch (start us, length us, event | category | flops | bytes accessed | tf_op | source)
XLA Modules:
  0.0 482.9 jit_solution(10885012108823817912)
XLA Ops:
  6.5 0.7 all-gather.5.cloned.1.call-update
  7.3 0.7 all-gather.3.cloned.1.call-update
  8.0 0.8 reshape.476
  8.9 5.6 %fusion.89 = (bf16[1,1024,1024]{2,1,0:T(8,128)(2,1)}, bf16[1,1024,1024]{2,1,0:T(8,128)(2,1)}, bf16[1,1024,1024]{2,1,0:T(8,128)(2,1)}, bf16[1,1024,1024]{2,1,0:T(8,128)(2,1)S(1)}) fusion(bf16[4,1024,1024]{2,1,0:T(8,128)(2,1)} %param.19), kind=kLoop, calls=%fused_computation.195 | loop fusion | bytes 16777216 | tf_op jit(solution)/shard_map/slice | solution.py:144
  14.6 2.6 copy.114
  17.1 2.9 copy.111
  20.0 0.6 gather_fusion
  20.7 0.6 gather_fusion.1
  21.4 0.7 fusion.99
  23.8 0.7 add_convert_fusion.8
  24.7 3.0 fusion.93
  27.8 1.5 fusion.92
  29.3 361.1 %all-gather.3.cloned.1.call-done = bf16[2048,4096]{1,0:T(8,128)(2,1)} async-done(((bf16[64,4096]{1,0:T(8,128)(2,1)}), bf16[2048,4096]{1,0:T(8,128)(2,1)}) %all-gather.3.cloned.1.call-update) | async-done | bytes 16777232 | tf_op jit(solution)/shard_map/all_gather | solution.py:127
  390.4 11.8 %fusion.24 = bf16[2048,160]{0,1:T(8,128)(2,1)S(1)} fusion(bf16[2048,4096]{1,0:T(8,128)(2,1)} %all-gather.3.cloned.1.call-done, bf16[4096,160]{0,1:T(8,128)(2,1)} %all-gather.5.cloned.1.call-done, f32[160]{0:T(256)S(1)} %reshape.502), kind=kOutput, calls=%fused_computation.55 | convolution fusion | flops 2685009920 | bytes 18743936 | tf_op jit(solution)/shard_map/dot_general | solution.py:126
  402.2 1.3 copy.102
  403.5 4.9 %all-to-all-start = ((bf16[32,64,160]{2,1,0:T(8,128)(2,1)}), bf16[32,64,160]{2,1,0:T(8,128)(2,1)}, u32[]{:S(2)}, u32[]{:S(2)}) async-start(bf16[32,64,160]{2,1,0:T(8,128)(2,1)} %bitcast.12), calls=%async_computation | async-start | bytes 2097152 | tf_op jit(solution)/shard_map/all_to_all | solution.py:132
  408.4 2.6 copy.108
  410.9 2.9 copy.105
  413.8 3.0 fusion.91
  416.8 1.1 fusion.90
  418.0 8.1 %all-to-all-done = bf16[32,64,160]{2,1,0:T(8,128)(2,1)} async-done(((bf16[32,64,160]{2,1,0:T(8,128)(2,1)}), bf16[32,64,160]{2,1,0:T(8,128)(2,1)}, u32[]{:S(2)}, u32[]{:S(2)}) %all-to-all-start) | async-done | bytes 655392 | tf_op jit(solution)/shard_map/all_to_all | solution.py:132
  426.1 1.6 reshape.477
  427.7 1.2 copy.180
  431.9 10.3 %while.71 = (s32[]{:T(128)}, f32[4,128]{1,0:T(4,128)S(1)}, f32[4,128]{1,0:T(4,128)S(1)}, f32[4,128,128]{2,1,0:T(8,128)S(1)}, s32[]{:T(128)}, /*index=5*/bf16[102...) while((s32[]{:T(128)}, f32[4,128]{1,0:T(4,128)S(1)}, ...), condition=%wide.region_23.25_spmd, body=%wide.region_20.24_spmd.sunk | while | flops 68158976 | bytes 3834551 | solution.py:99
  431.9 1.1 constant_dynamic-slice_fusion.15
  432.9 0.7 add_compare_fusion.11
  434.4 1.1 constant_dynamic-slice_fusion.15
  435.5 0.7 add_compare_fusion.11
  437.0 1.1 constant_dynamic-slice_fusion.15
  438.1 0.7 add_compare_fusion.11
  439.6 1.1 constant_dynamic-slice_fusion.15
  440.7 0.7 add_compare_fusion.11
  443.1 9.8 %while.70 = (s32[]{:T(128)}, f32[4,128]{1,0:T(4,128)S(1)}, f32[4,128]{1,0:T(4,128)S(1)}, f32[4,128,128]{2,1,0:T(8,128)S(1)}, s32[]{:T(128)}, /*index=5*/bf16[102...) while((s32[]{:T(128)}, f32[4,128]{1,0:T(4,128)S(1)}, ...), condition=%wide.region_17.19_spmd, body=%wide.region_14.18_spmd.sunk | while | flops 68158976 | bytes 3834551 | solution.py:99
  443.1 1.1 constant_dynamic-slice_fusion.14
  445.5 1.1 constant_dynamic-slice_fusion.14
  448.0 1.1 constant_dynamic-slice_fusion.14
  450.5 1.1 constant_dynamic-slice_fusion.14
  454.4 9.7 %while.69 = (s32[]{:T(128)}, f32[4,128]{1,0:T(4,128)S(1)}, f32[4,128]{1,0:T(4,128)S(1)}, f32[4,128,128]{2,1,0:T(8,128)S(1)}, s32[]{:T(128)}, /*index=5*/bf16[102...) while((s32[]{:T(128)}, f32[4,128]{1,0:T(4,128)S(1)}, ...), condition=%wide.region_11.13_spmd, body=%wide.region_8.12_spmd.sunk | while | flops 68158976 | bytes 3834551 | solution.py:99
  454.5 1.1 constant_dynamic-slice_fusion.13
  456.9 1.1 constant_dynamic-slice_fusion.13
  459.3 1.1 constant_dynamic-slice_fusion.13
  461.8 1.1 constant_dynamic-slice_fusion.13
  465.1 9.8 %while.68 = (s32[]{:T(128)}, f32[4,128]{1,0:T(4,128)S(1)}, f32[4,128]{1,0:T(4,128)S(1)}, f32[4,128,128]{2,1,0:T(8,128)S(1)}, s32[]{:T(128)}, /*index=5*/bf16[102...) while((s32[]{:T(128)}, f32[4,128]{1,0:T(4,128)S(1)}, ...), condition=%wide.region_5.7_spmd, body=%wide.region_2.6_spmd.sunk | while | flops 68158976 | bytes 3834551 | solution.py:99
  465.1 1.0 constant_dynamic-slice_fusion.12
  467.6 1.0 constant_dynamic-slice_fusion.12
  470.0 1.0 constant_dynamic-slice_fusion.12
  472.5 1.0 constant_dynamic-slice_fusion.12
  475.2 0.8 pad_maximum_fusion
  (190 shorter events, 27.4 us)
Async XLA Ops:
  6.5 13.5 %copy-start = (s32[256]{0:T(256)S(1)}, s32[256]{0:T(256)}, u32[]{:S(2)}) copy-start(s32[256]{0:T(256)} %param.21) | copy-start | bytes 3076
  6.5 22.7 %all-gather.5.cloned.1.call-start = ((), (), s32[]{:S(2)}) async-start(), calls=%async_computation.2 | async-start | bytes 1966080 | tf_op jit(solution)/shard_map/all_gather | solution.py:119
  7.3 383.1 %all-gather.3.cloned.1.call-start = ((), (), s32[]{:S(2)}) async-start(), calls=%async_computation.1 | async-start | bytes 17301504 | tf_op jit(solution)/shard_map/all_gather | solution.py:127
  17.1 3.6 copy-start.2
  402.2 6.2 %copy-start.3 = (bf16[1,1024,1024]{2,1,0:T(8,128)(2,1)S(1)}, bf16[1,1024,1024]{2,1,0:T(8,128)(2,1)}, u32[]{:S(2)}) copy-start(bf16[1,1024,1024]{2,1,0:T(8,128)(2,1)} %get-tuple-element.664) | copy-start | bytes 6291460
  403.5 22.6 %all-to-all-start = ((bf16[32,64,160]{2,1,0:T(8,128)(2,1)}), bf16[32,64,160]{2,1,0:T(8,128)(2,1)}, u32[]{:S(2)}, u32[]{:S(2)}) async-start(bf16[32,64,160]{2,1,0:T(8,128)(2,1)} %bitcast.12), calls=%async_computation | async-start | bytes 2097152 | tf_op jit(solution)/shard_map/all_to_all | solution.py:132
  474.9 1.1 copy-start.1
Sparse Core Ops, SparseCore 0:
  9.0 14.5 all-gather.4
  25.2 365.1 all-gather.2
where the time goes:
time: 484 us; the launch traced here: 483 us
  waiting for transfers between devices  371 us (77%)
  local copies, waits for them, and re-layouts  51.5 us (11%)
  matrix products  23.9 us (5%)
  other arithmetic  17 us (4%)
  between operations  13.9 us (3%)
  starting transfers between devices  4.9 us (1%)
    all_gather x1, waiting for transfers between devices, on_device(): lax.all_gather(tokens, 'grp', axis=0, tiled=True)  361 us
    dynamic_slice x16, local copies, waits for them, and re-layouts, visit(): lax.dynamic_slice_in_dim(value_part, offset, key_span, 0)  16.9 us
    dot_general x1, matrix products, on_device(): jnp.dot(lax.all_gather(tokens, 'grp', axis=0, tiled=True), weight_cols, p...  11.8 us
    unnamed x20, local copies, waits for them, and re-layouts  11.3 us
    lt x16, other arithmetic, visit(): in_cache = offset + jnp.arange(key_span, dtype=jnp.int32) < length  9.86 us
  transfers between devices with their start and end apart: 3, of which 2 were waited for; matrix products, arithmetic and copies ran while one was open for 6% of the time, Pallas kernels for 0%

commit v1 on v0

--- a/solution.py
+++ b/solution.py
@@ -10,6 +10,13 @@
 CAP = 1024
 GROUP = 8
 ROPE_THETA = 1000000.0
+
+
+def gather_over(block, axis, d):
+    devices = lax.axis_size(axis)
+    blocks = jnp.stack([block for _ in range(devices)])
+    blocks = lax.all_to_all(blocks, axis, split_axis=0, concat_axis=0)
+    return jnp.concatenate(blocks, axis=d)
 
 
 def rotate(vectors, positions):
@@ -124,9 +131,7 @@
         .astype(jnp.float32)
     )
     partial_cols = jnp.dot(
-        lax.all_gather(tokens, "grp", axis=0, tiled=True),
-        weight_cols,
-        preferred_element_type=jnp.float32,
+        gather_over(tokens, "grp", 0), weight_cols, preferred_element_type=jnp.float32
     )
     rounded_cols = (partial_cols + bias_cols[None, :]).astype(jnp.bfloat16)
     received = lax.all_to_all(rounded_cols, "grp", split_axis=0, concat_axis=1, tiled=True)

time: 484 us -> 406 us (0.84)
  waiting for transfers between devices: 371 us -> 236 us
  starting transfers between devices: 4.9 us -> 55.5 us
  local copies, waits for them, and re-layouts: 51.5 us -> 57.7 us
    all_gather x1 -> x0, waiting for transfers between devices: 361 us -> none  [on_device(): lax.all_gather(tokens, 'grp', axis=0, tiled=True)]
    all_to_all x0 -> x1, waiting for transfers between devices: none -> 229 us  [gather_over(): blocks = lax.all_to_all(blocks, axis, split_axis=0, concat_axis=0)]
    all_to_all x1, starting transfers between devices: 4.86 us -> 45.8 us  [on_device(): lax.all_to_all(rounded_cols, 'grp', split_axis=0, concat_axis=1, tiled=True)]
    all_to_all x0 -> x1, starting transfers between devices: none -> 9.61 us  [gather_over(): blocks = lax.all_to_all(blocks, axis, split_axis=0, concat_axis=0)]
    another operation x0 -> x1, local copies, waits for them, and re-layouts: none -> 6.74 us  [gather_over(): blocks = jnp.stack([block for _ in range(devices)])]
    unnamed x20 -> x22, local copies, waits for them, and re-layouts: 11.3 us -> 11.4 us
  transfers between devices with their start and end apart: 3 -> 3, of which waited for: 2 -> 2; matrix products, arithmetic and copies ran while one was open for 6% -> 7% of each run, Pallas kernels for 0% -> 0%
where the time goes in v1:
time: 406 us; the launch traced here: 405 us
  waiting for transfers between devices  236 us (58%)
  local copies, waits for them, and re-layouts  57.7 us (14%)
  starting transfers between devices  55.5 us (14%)
  matrix products  23.9 us (6%)
  other arithmetic  16.9 us (4%)
  between operations  13.9 us (3%)
    all_to_all x1, waiting for transfers between devices, gather_over(): blocks = lax.all_to_all(blocks, axis, split_axis=0, concat_axis=0)  229 us
    all_to_all x1, starting transfers between devices, on_device(): lax.all_to_all(rounded_cols, 'grp', split_axis=0, concat_axis=1, tiled=True)  45.8 us
    dynamic_slice x16, local copies, waits for them, and re-layouts, visit(): lax.dynamic_slice_in_dim(value_part, offset, key_span, 0)  16.9 us
    dot_general x1, matrix products, on_device(): jnp.dot(gather_over(tokens, 'grp', 0), weight_cols, preferred_element_typ...  11.8 us
    unnamed x22, local copies, waits for them, and re-layouts  11.4 us
    lt x16, other arithmetic, visit(): in_cache = offset + jnp.arange(key_span, dtype=jnp.int32) < length  9.74 us
    all_to_all x1, starting transfers between devices, gather_over(): blocks = lax.all_to_all(blocks, axis, split_axis=0, concat_axis=0)  9.61 us
    slice x4, local copies, waits for them, and re-layouts, attend(): value_part = slot_cache[:, kv_width:]  8.68 us
  transfers between devices with their start and end apart: 3, of which 2 were waited for; matrix products, arithmetic and copies ran while one was open for 7% of the time, Pallas kernels for 0%

profile of v1, /device:TPU:0, one launch (start us, length us, event | category | flops | bytes accessed | tf_op | source)
XLA Modules:
  0.0 405.1 jit_solution(2733757657523378965)
XLA Ops:
  6.5 6.7 %stack.2 = bf16[32,64,4096]{2,1,0:T(8,128)(2,1)} broadcast(bf16[64,4096]{1,0:T(8,128)(2,1)} %param.16), dimensions={1,2} | broadcast | bytes 17301504 | tf_op jit(solution)/shard_map/stack | solution.py:17
  13.3 9.6 %all-to-all-start = ((bf16[32,64,4096]{2,1,0:T(8,128)(2,1)}), bf16[32,64,4096]{2,1,0:T(8,128)(2,1)}, u32[]{:S(2)}, u32[]{:S(2)}) async-start(bf16[32,64,4096]{2,1,0:T(8,128)(2,1)} %stack.2), calls=%async_computation | async-start | bytes 33554432 | tf_op jit(solution)/shard_map/all_to_all | solution.py:18
  22.9 0.7 all-gather.2.cloned.1.call-update
  23.7 0.6 gather_fusion
  24.3 0.6 gather_fusion.1
  25.0 0.7 fusion.99
  25.7 5.8 %fusion.89 = (bf16[1,1024,1024]{2,1,0:T(8,128)(2,1)}, bf16[1,1024,1024]{2,1,0:T(8,128)(2,1)}, bf16[1,1024,1024]{2,1,0:T(8,128)(2,1)}, bf16[1,1024,1024]{2,1,0:T(8,128)(2,1)S(1)}) fusion(bf16[4,1024,1024]{2,1,0:T(8,128)(2,1)} %param.19), kind=kLoop, calls=%fused_computation.195 | loop fusion | bytes 16777216 | tf_op jit(solution)/shard_map/slice | solution.py:149
  31.7 2.6 copy.114
  34.2 3.0 copy.111
  38.4 0.7 add_convert_fusion.9
  39.9 3.0 fusion.93
  42.9 1.5 fusion.92
  44.4 228.7 %all-to-all-done = bf16[32,64,4096]{2,1,0:T(8,128)(2,1)} async-done(((bf16[32,64,4096]{2,1,0:T(8,128)(2,1)}), bf16[32,64,4096]{2,1,0:T(8,128)(2,1)}, u32[]{:S(2)}, u32[]{:S(2)}) %all-to-all-start) | async-done | bytes 16777248 | tf_op jit(solution)/shard_map/all_to_all | solution.py:18
  273.1 11.8 %fusion.24 = bf16[2048,160]{0,1:T(8,128)(2,1)S(1)} fusion(bf16[2048,4096]{1,0:T(8,128)(2,1)} %bitcast.12, bf16[4096,160]{0,1:T(8,128)(2,1)} %all-gather.2.cloned.1.call-done, f32[160]{0:T(256)S(1)} %reshape.508), kind=kOutput, calls=%fused_computation.55 | convolution fusion | flops 2685009920 | bytes 18743936 | tf_op jit(solution)/shard_map/dot_general | solution.py:133
  284.9 1.3 copy.102
  286.2 45.8 %all-to-all-start.1 = ((bf16[32,64,160]{2,1,0:T(8,128)(2,1)}), bf16[32,64,160]{2,1,0:T(8,128)(2,1)}, u32[]{:S(2)}, u32[]{:S(2)}) async-start(bf16[32,64,160]{2,1,0:T(8,128)(2,1)} %bitcast.13), calls=%async_computation.1 | async-start | bytes 2097152 | tf_op jit(solution)/shard_map/all_to_all | solution.py:137
  332.0 2.6 copy.108
  334.6 2.9 copy.105
  337.5 3.0 fusion.91
  340.5 1.1 fusion.90
  341.6 6.8 %all-to-all-done.1 = bf16[32,64,160]{2,1,0:T(8,128)(2,1)} async-done(((bf16[32,64,160]{2,1,0:T(8,128)(2,1)}), bf16[32,64,160]{2,1,0:T(8,128)(2,1)}, u32[]{:S(2)}, u32[]{:S(2)}) %all-to-all-start.1) | async-done | bytes 655392 | tf_op jit(solution)/shard_map/all_to_all | solution.py:137
  348.5 1.6 reshape.483
  350.1 1.2 copy.180
  354.2 9.8 %while.71 = (s32[]{:T(128)}, f32[4,128]{1,0:T(4,128)S(1)}, f32[4,128]{1,0:T(4,128)S(1)}, f32[4,128,128]{2,1,0:T(8,128)S(1)}, s32[]{:T(128)}, /*index=5*/bf16[102...) while((s32[]{:T(128)}, f32[4,128]{1,0:T(4,128)S(1)}, ...), condition=%wide.region_23.25_spmd, body=%wide.region_20.24_spmd.sunk | while | flops 68158976 | bytes 3834551 | solution.py:106
  354.2 1.1 constant_dynamic-slice_fusion.15
  356.7 1.1 constant_dynamic-slice_fusion.15
  359.1 1.1 constant_dynamic-slice_fusion.15
  361.6 1.1 constant_dynamic-slice_fusion.15
  364.9 10.3 %while.70 = (s32[]{:T(128)}, f32[4,128]{1,0:T(4,128)S(1)}, f32[4,128]{1,0:T(4,128)S(1)}, f32[4,128,128]{2,1,0:T(8,128)S(1)}, s32[]{:T(128)}, /*index=5*/bf16[102...) while((s32[]{:T(128)}, f32[4,128]{1,0:T(4,128)S(1)}, ...), condition=%wide.region_17.19_spmd, body=%wide.region_14.18_spmd.sunk | while | flops 68158976 | bytes 3834551 | solution.py:106
  364.9 1.1 constant_dynamic-slice_fusion.14
  366.0 0.7 add_compare_fusion.10
  367.5 1.1 constant_dynamic-slice_fusion.14
  368.6 0.7 add_compare_fusion.10
  370.1 1.1 constant_dynamic-slice_fusion.14
  371.2 0.7 add_compare_fusion.10
  372.7 1.1 constant_dynamic-slice_fusion.14
  373.7 0.7 add_compare_fusion.10
  376.8 10.0 %while.69 = (s32[]{:T(128)}, f32[4,128]{1,0:T(4,128)S(1)}, f32[4,128]{1,0:T(4,128)S(1)}, f32[4,128,128]{2,1,0:T(8,128)S(1)}, s32[]{:T(128)}, /*index=5*/bf16[102...) while((s32[]{:T(128)}, f32[4,128]{1,0:T(4,128)S(1)}, ...), condition=%wide.region_11.13_spmd, body=%wide.region_8.12_spmd.sunk | while | flops 68158976 | bytes 3834551 | solution.py:106
  376.8 1.1 constant_dynamic-slice_fusion.13
  379.3 1.1 constant_dynamic-slice_fusion.13
  381.8 1.1 constant_dynamic-slice_fusion.13
  384.3 1.1 constant_dynamic-slice_fusion.13
  387.7 9.5 %while.68 = (s32[]{:T(128)}, f32[4,128]{1,0:T(4,128)S(1)}, f32[4,128]{1,0:T(4,128)S(1)}, f32[4,128,128]{2,1,0:T(8,128)S(1)}, s32[]{:T(128)}, /*index=5*/bf16[102...) while((s32[]{:T(128)}, f32[4,128]{1,0:T(4,128)S(1)}, ...), condition=%wide.region_5.7_spmd, body=%wide.region_2.6_spmd.sunk | while | flops 68158976 | bytes 3834551 | solution.py:106
  387.7 1.0 constant_dynamic-slice_fusion.12
  390.1 1.0 constant_dynamic-slice_fusion.12
  392.4 1.0 constant_dynamic-slice_fusion.12
  394.8 1.0 constant_dynamic-slice_fusion.12
  397.4 0.8 pad_maximum_fusion
  (192 shorter events, 27.4 us)
Async XLA Ops:
  6.5 17.1 %copy-start = (s32[256]{0:T(256)S(1)}, s32[256]{0:T(256)}, u32[]{:S(2)}) copy-start(s32[256]{0:T(256)} %param.21) | copy-start | bytes 3076
  13.3 11.1 %copy-start.2 = (s32[256]{0:T(256)S(1)}, s32[256]{0:T(256)}, u32[]{:S(2)}) copy-start(s32[256]{0:T(256)} %param.20) | copy-start | bytes 3076
  13.3 259.8 %all-to-all-start = ((bf16[32,64,4096]{2,1,0:T(8,128)(2,1)}), bf16[32,64,4096]{2,1,0:T(8,128)(2,1)}, u32[]{:S(2)}, u32[]{:S(2)}) async-start(bf16[32,64,4096]{2,1,0:T(8,128)(2,1)} %stack.2), calls=%async_computation | async-start | bytes 33554432 | tf_op jit(solution)/shard_map/all_to_all | solution.py:18
  22.9 21.5 %all-gather.2.cloned.1.call-start = ((), (), s32[]{:S(2)}) async-start(), calls=%async_computation.2 | async-start | bytes 1966080 | tf_op jit(solution)/shard_map/all_gather | solution.py:126
  25.7 5.8 %copy-start.4 = (bf16[5120]{0:T(1024)(128)(2,1)S(1)}, bf16[5120]{0:T(1024)(128)(2,1)}, u32[]{:S(2)}) copy-start(bf16[5120]{0:T(1024)(128)(2,1)} %param.18) | copy-start | bytes 30724
  284.9 47.2 %copy-start.3 = (bf16[1,1024,1024]{2,1,0:T(8,128)(2,1)S(1)}, bf16[1,1024,1024]{2,1,0:T(8,128)(2,1)}, u32[]{:S(2)}) copy-start(bf16[1,1024,1024]{2,1,0:T(8,128)(2,1)} %get-tuple-element.664) | copy-start | bytes 6291460
  286.2 62.3 %all-to-all-start.1 = ((bf16[32,64,160]{2,1,0:T(8,128)(2,1)}), bf16[32,64,160]{2,1,0:T(8,128)(2,1)}, u32[]{:S(2)}, u32[]{:S(2)}) async-start(bf16[32,64,160]{2,1,0:T(8,128)(2,1)} %bitcast.13), calls=%async_computation.1 | async-start | bytes 2097152 | tf_op jit(solution)/shard_map/all_to_all | solution.py:137
  397.2 1.1 copy-start.1
Sparse Core Ops, SparseCore 0:
  25.4 13.1 all-gather.1
